TPU v7x, 768 devices: a whole 4x8x12 slice. The times are simulated.
768 devices in a mesh: row: 16 (over y, core), col: 48 (over z, x).
Axes of the slice: x: 4, y: 8, z: 12, core: 2. Of those that a mesh axis runs over, the one named last changes fastest.
Arguments:
- panel: bfloat16 [98304, 128], P(('row', 'col')), may hold values from -6 to 6
- previous: bfloat16 [98304, 128], P(('row', 'col')), may hold values from -6 to 6
- blocks: bfloat16 [16, 48, 64, 128, 128], P('row', 'col'), may hold values from -0.046875 to 0.046875
- block_rows: int32 [16, 48, 64], P('row', 'col'), may hold values from 0 to 47
- block_cols: int32 [16, 48, 64], P('row', 'col'), may hold values from 0 to 15
- counts: int32 [16, 48], P('row', 'col'), may hold values from 8 to 64, as said below
- center: float32 [1], replicated, may hold values from -0.5 to 0.5
- half_width: float32 [1], replicated, may hold values from 1 to 2
Outputs:
- filtered: bfloat16 [98304, 128], P(('row', 'col'))
Inputs may be any that keep to these rules, and one draw needn't show every extreme that they name: `counts`: live slots of each device; some device has all 64 slots live.
All inputs are finite; a program needn't handle non-finite values.
Results may differ from a plain program's by a relative error of at most 0.014.
Values may be sent and summed in bfloat16 or wider, within the bound.
A program may use at most 32 MiB of HBM per device.

v0:
```python
import jax
import jax.numpy as jnp
from jax import lax
from jax.sharding import PartitionSpec as P


def body(panel, previous, blocks, block_rows, block_cols, counts, center, half_width):
    tile_size = blocks.shape[-1]
    vec_width = panel.shape[-1]
    stored = blocks.reshape(blocks.shape[2:])
    slot_count = stored.shape[0]
    rows_here = block_rows.reshape(slot_count)
    cols_here = block_cols.reshape(slot_count)
    live_mask = (jnp.arange(slot_count, dtype=jnp.int32) < counts.reshape(())).astype(jnp.bfloat16)
    row_group = lax.all_gather(panel, "col", axis=0, tiled=True).reshape(-1, tile_size, vec_width)
    col_group = lax.all_gather(panel, "row", axis=0, tiled=True).reshape(-1, tile_size, vec_width)
    direct = jnp.einsum(
        "sab,sbk->sak", stored, col_group[cols_here], preferred_element_type=jnp.float32
    ).reshape(slot_count, -1)
    mirror = jnp.einsum(
        "sba,sbk->sak", stored, row_group[rows_here], preferred_element_type=jnp.float32
    ).reshape(slot_count, -1)

    def split_parts(products):
        upper_part = products.astype(jnp.bfloat16)
        lower_part = (products - upper_part.astype(jnp.float32)).astype(jnp.bfloat16)
        return (upper_part, lower_part)

    direct_parts = split_parts(direct)
    mirror_parts = split_parts(mirror)

    def collect(parts, targets, block_count):
        selector = (targets[None, :] == jnp.arange(block_count, dtype=jnp.int32)[:, None]).astype(
            jnp.bfloat16
        )
        selector = selector * live_mask[None, :]
        summed = jnp.dot(selector, parts[0], preferred_element_type=jnp.float32)
        summed = summed + jnp.dot(selector, parts[1], preferred_element_type=jnp.float32)
        return summed.reshape(block_count * tile_size, vec_width)

    row_sums = lax.psum_scatter(
        collect(direct_parts, rows_here, row_group.shape[0]), "col", scatter_dimension=0, tiled=True
    )
    mirrored = lax.psum_scatter(
        collect(mirror_parts, cols_here, col_group.shape[0]).astype(jnp.bfloat16),
        "row",
        scatter_dimension=0,
        tiled=True,
    ).astype(jnp.float32)
    product = row_sums + mirrored
    result = 2.0 / half_width[0] * (
        product - center[0] * panel.astype(jnp.float32)
    ) - previous.astype(jnp.float32)
    return result.astype(jnp.bfloat16)


def solution(mesh):
    placed = (
        P(("row", "col"), None),
        P(("row", "col"), None),
        P("row", "col", None, None, None),
        P("row", "col", None),
        P("row", "col", None),
        P("row", "col"),
        P(),
        P(),
    )
    return jax.shard_map(
        body, mesh=mesh, in_specs=placed, out_specs=P(("row", "col"), None), check_vma=False
    )
```

profile of v0, /device:TPU:1, one launch (start us, length us, event | category | flops | bytes accessed | tf_op | source)
XLA Modules:
  0.0 653.4 jit_solution(12804549026255564590)
XLA Ops:
  6.5 0.0 copy-start
  6.5 0.0 all-gather.2.cloned.1.call-start
  6.5 0.7 all-gather.2.cloned.1.call-update
  7.3 0.0 reduce-scatter.5.cloned.1.call-start
  8.0 0.7 fusion.27
  8.6 26.3 %all_gather.6 = bf16[2048,128]{1,0:T(8,128)(2,1)S(1)} all-gather(bf16[128,128]{1,0:T(8,128)(2,1)} %param.8), channel_id=1, replica_groups=mesh['row'=16,'col'=48] {'row'}, dimensions={0}, use_global_device_ids=true | all-gather | bytes 557056 | tf_op jit(solution)/shard_map/all_gather | solution.py:16
  34.9 0.0 copy-start.5
  34.9 2.2 gather_fusion
  37.1 0.0 copy-done.5
  37.1 91.1 %all-gather.2.cloned.1.call-done = bf16[6144,128]{1,0:T(8,128)(2,1)} async-done(((bf16[128,128]{1,0:T(8,128)(2,1)}), bf16[6144,128]{1,0:T(8,128)(2,1)}) %all-gather.2.cloned.1.call-update) | async-done | bytes 1572880 | tf_op jit(solution)/shard_map/all_gather | solution.py:15
  128.2 3.5 gather_fusion.1
  131.7 0.0 copy-done
  131.7 4.4 convolution_bitcast_fusion
  136.1 0.0 copy-start.4
  136.1 5.6 copy.12
  141.8 0.0 copy-done.4
  141.8 4.5 fusion.4
  146.3 4.5 fusion
  150.8 1.1 convert_element_type.53
  151.9 0.0 reduce-scatter.5.cloned.1.call-update
  151.9 0.2 reduce-scatter.3.cloned.1.call-start
  152.1 5.2 convolution_bitcast_fusion.1
  157.3 5.6 copy.10
  162.9 0.0 copy-start.1
  162.9 5.1 fusion.3
  168.0 0.0 copy-done.1
  168.0 4.5 convolution_add_fusion
  172.5 4.5 reshape.99
  177.1 0.0 copy-start.2
  177.1 0.0 copy-start.3
  177.1 0.0 reduce-scatter.3.cloned.1.call-update
  178.4 37.1 %reduce-scatter.5.cloned.1.call-done = bf16[128,128]{1,0:T(8,128)(2,1)} async-done(((bf16[2048,128]{1,0:T(8,128)(2,1)}), bf16[128,128]{1,0:T(8,128)(2,1)}) %reduce-scatter.5.cloned.1.call-update) | async-done | bytes 32784 | tf_op jit(solution)/shard_map/reduce_scatter | solution.py:44
  215.5 429.9 %reduce-scatter.3.cloned.1.call-done = f32[128,128]{1,0:T(8,128)} async-done(((f32[6144,128]{1,0:T(8,128)}), f32[128,128]{1,0:T(8,128)}) %reduce-scatter.3.cloned.1.call-update) | async-done | bytes 65552 | tf_op jit(solution)/shard_map/reduce_scatter | solution.py:41
  645.4 0.0 copy-done.2
  645.4 0.0 copy-done.3
  645.4 1.5 subtract_convert_fusion
  (4 shorter events, 0.0 us)
Async XLA Ops:
  6.5 125.2 %copy-start = (bf16[1,1,64,128,128]{4,3,2,1,0:T(8,128)(2,1)S(1)}, bf16[1,1,64,128,128]{4,3,2,1,0:T(8,128)(2,1)}, u32[]{:S(2)}) copy-start(bf16[1,1,64,128,128]{4,3,2,1,0:T(8,128)(2,1)} %param.10) | copy-start | bytes 6291460
  6.5 121.7 %all-gather.2.cloned.1.call-start = ((), (), s32[]{:S(2)}) async-start(), calls=%async_computation.3 | async-start | bytes 1605632 | tf_op jit(solution)/shard_map/all_gather | solution.py:15
  7.3 208.3 %reduce-scatter.5.cloned.1.call-start = ((), (), s32[]{:S(2)}) async-start(), calls=%async_computation.4 | async-start | bytes 557056 | tf_op jit(solution)/shard_map/reduce_scatter | solution.py:44
  34.9 2.2 copy-start.5
  136.1 5.6 copy-start.4
  151.9 493.5 %reduce-scatter.3.cloned.1.call-start = ((), (), s32[]{:S(2)}) async-start(), calls=%async_computation.2 | async-start | bytes 3211264 | tf_op jit(solution)/shard_map/reduce_scatter | solution.py:41
  162.9 5.1 copy-start.1
  177.1 468.3 %copy-start.2 = (bf16[128,128]{1,0:T(8,128)(2,1)S(1)}, bf16[128,128]{1,0:T(8,128)(2,1)}, u32[]{:S(2)}) copy-start(bf16[128,128]{1,0:T(8,128)(2,1)} %param.8) | copy-start | bytes 98308
  177.1 468.3 %copy-start.3 = (bf16[128,128]{1,0:T(8,128)(2,1)S(1)}, bf16[128,128]{1,0:T(8,128)(2,1)}, u32[]{:S(2)}) copy-start(bf16[128,128]{1,0:T(8,128)(2,1)} %param.9) | copy-start | bytes 98308
Sparse Core Ops, SparseCore 0:
  10.9 117.2 all-gather.1
  152.0 63.4 reduce-scatter.4
  221.4 423.9 reduce-scatter.2
where the time goes:
time: 661 us; the launch traced here: 653 us
  waiting for transfers between devices  559 us (85%)
  matrix products  28.2 us (4%)
  blocking collectives  26.3 us (4%)
  local copies, waits for them, and re-layouts  22.6 us (3%)
  between operations  15.1 us (2%)
    reduce_scatter x1, waiting for transfers between devices, body(): lax.psum_scatter(collect(direct_parts, rows_here, row_group.shape[0]), 'c...  430 us
    all_gather x1, waiting for transfers between devices, body(): lax.all_gather(panel, 'col', axis=0, tiled=True)  91.1 us
    reduce_scatter x1, waiting for transfers between devices, body(): lax.psum_scatter(collect(mirror_parts, cols_here, col_group.shape[0]).ast...  37.1 us
    all_gather x1, blocking collectives, body(): lax.all_gather(panel, 'row', axis=0, tiled=True)  26.3 us
  transfers between devices with their start and end apart: 3, of which 3 were waited for; matrix products, arithmetic and copies ran while one was open for 4% of the time, Pallas kernels for 0%

commit v1 on v0

v1 whole, which is shorter than its diff:
```python
import functools

import jax
import jax.numpy as jnp
from jax import lax
from jax.experimental import pallas as pl
from jax.experimental.pallas import tpu as pltpu
from jax.sharding import PartitionSpec as P

MESH = pl.DeviceIdType.MESH
BF = jnp.bfloat16
F32 = jnp.float32
NX = 4
NR = 3


def kernel(nx, ny, ns, half, tab, center, width, panel, previous, blocks_hbm, out,
           C, G, B, D, M, T, RXA, RZB, RZA, RXB, SA, SB, S3, SH, R3, MS, MR, N, YR,
           bsem, cs, cr, gs, gr, rs, rr, ms, mr):
    row = lax.axis_index("row")
    col = lax.axis_index("col")
    y, k = row // 2, row % 2
    z, x = col // nx, col % nx
    zs, zr = z // NR, z % NR
    nz = ns * NR
    slots = B.shape[0]
    bs = panel.shape[0]
    zm, zp = (zr + NR - 1) % NR, (zr + 1) % NR
    o_ck, o_pr, o_lr, o_pc, o_lc = slots, 2 * slots, 3 * slots, 3 * slots + nz * nx, 4 * slots + nz * nx

    def at(dy=0, dk=0, dz=0, dx=0):
        return {
            "row": ((y + dy) % ny) * 2 + (k + dk) % 2,
            "col": ((z + dz) % nz) * nx + (x + dx) % nx,
        }

    started = []

    def send(src, dst, ssem, rsem, dev):
        cp = pltpu.make_async_remote_copy(
            src_ref=src, dst_ref=dst, send_sem=ssem, recv_sem=rsem, device_id=dev, device_id_type=MESH
        )
        cp.start()
        started.append(cp)

    def got(dst, rsem):
        pltpu.make_async_remote_copy(
            src_ref=dst, dst_ref=dst, send_sem=rsem, recv_sem=rsem, device_id=at(), device_id_type=MESH
        ).wait_recv()

    block_copy = pltpu.make_async_copy(blocks_hbm, B, bsem)
    block_copy.start()

    peers = [at(dk=1)]
    peers += [at(dy=d) for d in range(1, ny)]
    peers += [at(dz=NR * d) for d in range(1, ns)]
    peers += [at(dz=1), at(dz=-1)]
    peers += [at(dx=d) for d in range(1, nx)]
    barrier = pltpu.get_barrier_semaphore()
    for dev in peers:
        pl.semaphore_signal(barrier, inc=1, device_id=dev, device_id_type=MESH)
    own = panel[...]
    C[k * ny + y] = own
    G[zr, zs, x] = own.astype(F32).T.astype(BF)
    D[slots] = jnp.zeros(D.shape[1:], F32)
    M[slots] = jnp.zeros(M.shape[1:], F32)
    pl.semaphore_wait(barrier, len(peers))

    for d in range(1, ny):
        send(C.at[k * ny + y], C.at[k * ny + y], cs.at[d], cr.at[d], at(dy=d))
    send(C.at[k * ny + y], C.at[k * ny + y], cs.at[0], cr.at[0], at(dk=1))
    for d in range(1, ns):
        send(G.at[zr, zs, x], G.at[zr, zs, x], gs.at[0, d], gr.at[0, d], at(dz=NR * d))
    for d in range(1, ns):
        got(G.at[zr, zs, x], gr.at[0, d])
    for e, dz in enumerate((1, -1)):
        send(G.at[zr, :, x], G.at[zr, :, x], gs.at[1, e], gr.at[1, e], at(dz=dz))
    for d in range(1, nx):
        send(G.at[zr, :, x], G.at[zr, :, x], gs.at[2, d], gr.at[2, d], at(dx=d))

    for d in range(1, ny):
        got(C.at[k * ny + y], cr.at[d])
        there = C.at[k * ny + (y + ny - d) % ny]
        send(there, there, cs.at[ny + d], cr.at[ny + d], at(dk=1))

    for e, q in enumerate((zm, zp)):
        got(G.at[zr, :, x], gr.at[1, e])
        for d in range(1, nx):
            part = G.at[q, :, x, pl.ds(0, half)]
            send(part, part, gs.at[3 + e, d], gr.at[3 + e, d], at(dx=d))
    for d in range(1, nx):
        got(G.at[zr, :, x], gr.at[2, d])
        for e, dz in enumerate((1, -1)):
            part = G.at[zr, :, (x + nx - d) % nx, pl.ds(half, bs - half)]
            send(part, part, gs.at[5 + e, d], gr.at[5 + e, d], at(dz=dz))

    block_copy.wait()
    got(C.at[k * ny + y], cr.at[0])
    for d in range(1, ny):
        got(C.at[k * ny + y], cr.at[ny + d])

    def direct(s, carry):
        p = C[tab[o_ck + s]]
        D[s] = jnp.dot(B[s], p, preferred_element_type=F32) + D[tab[o_pr + s]]
        return carry

    lax.fori_loop(0, slots, direct, 0, unroll=8)

    def round_rows(i, carry):
        T[i // (ns * nx), (i // nx) % ns, i % nx] = D[tab[o_lr + i]].astype(BF)
        return carry

    lax.fori_loop(0, nz * nx, round_rows, 0, unroll=4)
    for d in range(1, nx):
        send(T.at[:, :, (x + d) % nx, pl.ds(0, half)], RXA.at[d - 1], rs.at[0, d], rr.at[0, d], at(dx=d))
    for e, (q, dz) in enumerate(((zp, 1), (zm, -1))):
        send(T.at[q, :, :, pl.ds(half, bs - half)], RZB.at[e], rs.at[1, e], rr.at[1, e], at(dz=dz))

    for e in range(2):
        for d in range(1, nx):
            got(G.at[zr, :, x, pl.ds(0, half)], gr.at[3 + e, d])
            got(G.at[zr, :, x, pl.ds(half, bs - half)], gr.at[5 + e, d])

    def mirror(s, carry):
        t = tab[s]
        p = G[lax.div(t, ns * nx), lax.rem(lax.div(t, nx), ns), lax.rem(t, nx)]
        M[s] = jnp.dot(p, B[s], preferred_element_type=F32) + M[tab[o_pc + s]]
        return carry

    lax.fori_loop(0, slots, mirror, 0, unroll=8)

    def round_other(i, carry):
        MS[i] = M[tab[o_lc + (1 - k) * ny + i]].astype(BF)
        return carry

    lax.fori_loop(0, ny, round_other, 0, unroll=4)
    send(MS, MR, ms.at[0], mr.at[0], at(dk=1))

    for e in range(2):
        got(RZB.at[e], rr.at[1, e])

    def sum_b(i, carry):
        s, w = i // nx, i % nx
        total = D[tab[o_lr + (zr * ns + s) * nx + w]][half:]
        total = total + RZB[0, s, w].astype(F32) + RZB[1, s, w].astype(F32)
        SB[w, s] = total.astype(BF)
        return carry

    lax.fori_loop(0, ns * nx, sum_b, 0, unroll=4)
    for d in range(1, nx):
        send(SB.at[(x + d) % nx], RXB.at[d - 1], rs.at[2, d], rr.at[2, d], at(dx=d))
    for d in range(1, nx):
        got(RXA.at[d - 1], rr.at[0, d])

    def sum_a(i, carry):
        q, s = i // ns, i % ns
        total = D[tab[o_lr + i * nx + x]][:half]
        for d in range(1, nx):
            total = total + RXA[d - 1, q, s].astype(F32)
        SA[q, s] = total.astype(BF)
        return carry

    lax.fori_loop(0, NR * ns, sum_a, 0, unroll=4)
    for e, (q, dz) in enumerate(((zp, 1), (zm, -1))):
        send(SA.at[q], RZA.at[e], rs.at[3, e], rr.at[3, e], at(dz=dz))

    got(MR, mr.at[0])

    def sum_m(i, carry):
        N[i] = (M[tab[o_lc + k * ny + i]] + MR[i].astype(F32)).astype(BF)
        return carry

    lax.fori_loop(0, ny, sum_m, 0, unroll=4)
    for d in range(1, ny):
        send(N.at[(y + d) % ny], YR.at[d - 1], ms.at[d], mr.at[d], at(dy=d))

    for e in range(2):
        got(RZA.at[e], rr.at[3, e])
    for d in range(1, nx):
        got(RXB.at[d - 1], rr.at[2, d])

    def sum_3(s, carry):
        a = SA[zr, s].astype(F32) + RZA[0, s].astype(F32) + RZA[1, s].astype(F32)
        b = SB[x, s].astype(F32)
        for d in range(1, nx):
            b = b + RXB[d - 1, s].astype(F32)
        S3[s, :half] = a
        S3[s, half:] = b
        SH[s, :half] = a.astype(BF)
        SH[s, half:] = b.astype(BF)
        return carry

    lax.fori_loop(0, ns, sum_3, 0, unroll=ns)
    for d in range(1, ns):
        send(SH.at[(zs + d) % ns], R3.at[d - 1], rs.at[4, d], rr.at[4, d], at(dz=NR * d))

    total = M[tab[o_lc + k * ny + y]] + MR[y].astype(F32)
    for d in range(1, ny):
        got(YR.at[d - 1], mr.at[d])
        total = total + YR[d - 1].astype(F32)
    product = total.T + S3[zs]
    scale = 2.0 / jnp.full((bs, bs), width[0], F32)
    shift = center[0] * panel[...].astype(F32)
    before = previous[...].astype(F32)
    for d in range(1, ns):
        got(R3.at[d - 1], rr.at[4, d])
        product = product + R3[d - 1].astype(F32)
    out[...] = (scale * (product - shift) - before).astype(BF)
    for cp in started:
        cp.wait_send()


def body(nx, panel, previous, blocks, block_rows, block_cols, counts, center, half_width):
    bs = panel.shape[0]
    ny = lax.axis_size("row") // 2
    ncol = lax.axis_size("col")
    nz = ncol // nx
    ns = nz // NR
    slots = blocks.shape[2]
    half = bs // 2
    rows = block_rows.reshape(slots)
    cols = block_cols.reshape(slots)
    count = counts.reshape(())
    zi = rows // nx
    rk = ((zi % NR) * ns + zi // NR) * nx + rows % nx
    ck = (cols % 2) * ny + cols // 2
    place = jnp.arange(slots, dtype=jnp.int32)
    full = jnp.broadcast_to(count, (ncol,))
    want = jnp.concatenate([rk, jnp.arange(ncol, dtype=jnp.int32), ck, jnp.arange(2 * ny, dtype=jnp.int32)])
    limit = jnp.concatenate([place, full, place, full[: 1].repeat(2 * ny)])
    is_row = jnp.arange(want.shape[0]) < slots + ncol
    keys = jnp.where(is_row[:, None], rk[None, :], ck[None, :])
    hit = (keys == want[:, None]) & (place[None, :] < limit[:, None])
    found = jnp.max(jnp.where(hit, place[None, :], -1), axis=1)
    found = jnp.where(found < 0, slots, found)
    tab = jnp.concatenate([rk, ck, found])

    smem = pl.BlockSpec(memory_space=pltpu.SMEM)
    vmem = pl.BlockSpec(memory_space=pltpu.VMEM)
    dma = pltpu.SemaphoreType.DMA
    rest = bs - half
    return pl.pallas_call(
        functools.partial(kernel, nx, ny, ns, half),
        name="filter_step",
        out_shape=jax.ShapeDtypeStruct((bs, bs), BF),
        in_specs=[smem, smem, smem, vmem, vmem, pl.BlockSpec(memory_space=pl.ANY)],
        out_specs=vmem,
        scratch_shapes=[
            pltpu.VMEM((2 * ny, bs, bs), BF),
            pltpu.VMEM((NR, ns, nx, bs, bs), BF),
            pltpu.VMEM((slots, bs, bs), BF),
            pltpu.VMEM((slots + 1, bs, bs), F32),
            pltpu.VMEM((slots + 1, bs, bs), F32),
            pltpu.VMEM((NR, ns, nx, bs, bs), BF),
            pltpu.VMEM((nx - 1, NR, ns, half, bs), BF),
            pltpu.VMEM((2, ns, nx, rest, bs), BF),
            pltpu.VMEM((2, ns, half, bs), BF),
            pltpu.VMEM((nx - 1, ns, rest, bs), BF),
            pltpu.VMEM((NR, ns, half, bs), BF),
            pltpu.VMEM((nx, ns, rest, bs), BF),
            pltpu.VMEM((ns, bs, bs), F32),
            pltpu.VMEM((ns, bs, bs), BF),
            pltpu.VMEM((max(ns - 1, 1), bs, bs), BF),
            pltpu.VMEM((ny, bs, bs), BF),
            pltpu.VMEM((ny, bs, bs), BF),
            pltpu.VMEM((ny, bs, bs), BF),
            pltpu.VMEM((ny - 1, bs, bs), BF),
            dma,
            dma((2 * ny,)), dma((2 * ny,)),
            dma((7, 4)), dma((7, 4)),
            dma((5, 4)), dma((5, 4)),
            dma((ny,)), dma((ny,)),
        ],
        compiler_params=pltpu.CompilerParams(
            collective_id=0, has_side_effects=True, vmem_limit_bytes=48 << 20
        ),
    )(tab, center, half_width, panel, previous, blocks.reshape(slots, bs, bs))


def solution(mesh):
    placed = (
        P(("row", "col"), None),
        P(("row", "col"), None),
        P("row", "col", None, None, None),
        P("row", "col", None),
        P("row", "col", None),
        P("row", "col"),
        P(),
        P(),
    )
    return jax.shard_map(
        functools.partial(body, NX), mesh=mesh, in_specs=placed, out_specs=P(("row", "col"), None), check_vma=False
    )
```

time: 661 us -> 68.9 us (0.10)
  the two profiles are of different devices: /device:TPU:1 before, /device:TPU:2 now
where the time goes in v1:
time: 68.9 us; the launch traced here: 68.6 us
  Pallas kernels  61.8 us (90%)
  local copies, waits for them, and re-layouts  3.74 us (5%)
  between operations  2 us (3%)
  other arithmetic  1.04 us (2%)
    pallas_call x1, Pallas kernels, body(): pl.pallas_call(functools.partial(kernel, nx, ny, ns, half), name='filter_...  61.8 us
    unnamed x7, local copies, waits for them, and re-layouts  3.72 us

profile of v1, /device:TPU:2, one launch (start us, length us, event | category | flops | bytes accessed | tf_op | source)
XLA Modules:
  0.0 68.6 jit_solution(11593031654310556581)
XLA Ops:
  2.0 0.1 pad_add_fusion.2
  2.1 0.7 %fusion.1 = (s32[64]{0:T(128)S(1)}, s32[64]{0:T(128)S(1)}) fusion(s32[1,1,64]{2,1,0:T(1,128)} %param.11, s32[1,1,64]{2,1,0:T(1,128)} %param.12), kind=kLoop, calls=%fused_computation.21 | loop fusion | flops 3584 | bytes 1024 | tf_op jit(solution)/shard_map/add | solution.py:225
  2.8 0.1 pad_add_fusion.1
  2.8 0.1 select_reduce_fusion
  3.0 0.1 pad_add_fusion.tab
  3.0 0.0 copy-start
  3.0 1.6 %copy-done = bf16[1,1,64,128,128]{4,3,2,1,0:T(8,128)(2,1)S(1)} copy-done((bf16[1,1,64,128,128]{4,3,2,1,0:T(8,128)(2,1)S(1)}, bf16[1,1,64,128,128]{4,3,2,1,0:T(8,128)(2,1)}, u32[]{:S(2)}) %copy-start) | copy-done | bytes 2097176
  4.6 0.0 copy-start.1
  4.6 0.8 %copy-done.1 = bf16[128,128]{1,0:T(8,128)(2,1)S(1)} copy-done((bf16[128,128]{1,0:T(8,128)(2,1)S(1)}, bf16[128,128]{1,0:T(8,128)(2,1)}, u32[]{:S(2)}) %copy-start.1) | copy-done | bytes 32792
  5.4 0.0 copy-start.2
  5.4 0.8 %copy-done.2 = bf16[128,128]{1,0:T(8,128)(2,1)S(1)} copy-done((bf16[128,128]{1,0:T(8,128)(2,1)S(1)}, bf16[128,128]{1,0:T(8,128)(2,1)}, u32[]{:S(2)}) %copy-start.2) | copy-done | bytes 32792
  6.1 61.8 %filter_step.1 = bf16[128,128]{1,0:T(8,128)(2,1)S(1)} custom-call(s32[320]{0:T(512)S(1)} %pad_add_fusion.tab, f32[1]{0:T(128)S(6)} %copy.11.center, f32[1]{0:T(128)S(6)} %copy.12.width, bf16[128,128]{1,0:T(8,128)(2,1)S(1)} %copy-done.1, bf16[128,128]{1,0:T(8,128)(2,1)S(1)} %copy-done.2, bf16[64,128,128]{2,1,0:T(8,128)(2,1)S(1)} %bitcast.30), custom_call_target="tpu_custom_call" | custom-call | tf_op jit(solution)/shard_map/filter_step/pallas_call | solution.py:242
  68.0 0.6 copy.13
  (7 shorter events, 0.0 us)
Async XLA Ops:
  3.0 1.6 %copy-start = (bf16[1,1,64,128,128]{4,3,2,1,0:T(8,128)(2,1)S(1)}, bf16[1,1,64,128,128]{4,3,2,1,0:T(8,128)(2,1)}, u32[]{:S(2)}) copy-start(bf16[1,1,64,128,128]{4,3,2,1,0:T(8,128)(2,1)} %param.10) | copy-start | bytes 6291460
  4.6 0.8 %copy-start.1 = (bf16[128,128]{1,0:T(8,128)(2,1)S(1)}, bf16[128,128]{1,0:T(8,128)(2,1)}, u32[]{:S(2)}) copy-start(bf16[128,128]{1,0:T(8,128)(2,1)} %panel.1) | copy-start | bytes 98308
  5.4 0.8 %copy-start.2 = (bf16[128,128]{1,0:T(8,128)(2,1)S(1)}, bf16[128,128]{1,0:T(8,128)(2,1)}, u32[]{:S(2)}) copy-start(bf16[128,128]{1,0:T(8,128)(2,1)} %previous.1) | copy-start | bytes 98308

commit v2 on v0

v2 whole, which is shorter than its diff:
```python
import functools

import jax
import jax.numpy as jnp
from jax import lax
from jax.experimental import pallas as pl
from jax.experimental.pallas import tpu as pltpu
from jax.sharding import PartitionSpec as P

MESH = pl.DeviceIdType.MESH
BF = jnp.bfloat16
F32 = jnp.float32
I32 = jnp.int32
NX = 4
NR = 3
GATHER_ROWS = 64
REDUCE_ROWS = 48
UNROLL = 32


class Lane:
    def __init__(self, sends, recvs):
        self.sends, self.recvs, self.count, self.started = sends, recvs, 0, []

    def make(self, src, dst, dev):
        i, self.count = self.count, self.count + 1
        cp = pltpu.make_async_remote_copy(
            src_ref=src, dst_ref=dst, send_sem=self.sends.at[i], recv_sem=self.recvs.at[i],
            device_id=dev, device_id_type=MESH,
        )
        self.started.append(cp)
        return i, cp

    def send(self, src, dst, dev):
        i, cp = self.make(src, dst, dev)
        cp.start()
        return i

    def got(self, like, i, dev):
        pltpu.make_async_remote_copy(
            src_ref=like, dst_ref=like, send_sem=self.recvs.at[i], recv_sem=self.recvs.at[i],
            device_id=dev, device_id_type=MESH,
        ).wait_recv()

    def drain(self):
        for cp in self.started:
            cp.wait_send()


def kernel(nx, ny, ns, count, center, width, panel_hbm, previous_hbm, blocks_hbm, rows_hbm, cols_hbm, out,
           panel, previous, B, rows, cols, tabv, tab,
           C, G, D, M, T, RXA, RZB, RZA, RXB, SA, SB, S3, SH, R3, MS, MR, N, YR,
           lsem, cs, cr, gs, gr, rs, rr, ms, mr):
    row = lax.axis_index("row")
    col = lax.axis_index("col")
    y, k = row // 2, row % 2
    z, x = col // nx, col % nx
    zs, zr = z // NR, z % NR
    nz = ns * NR
    h = ns // 2
    par, pair = zs % 2, zs // 2
    slot = par * h + pair
    slots = B.shape[0]
    bs = panel.shape[0]
    zm, zp = (zr + NR - 1) % NR, (zr + 1) % NR
    ga, ra = GATHER_ROWS, REDUCE_ROWS
    lo, hi = pl.ds(0, ga), pl.ds(ga, bs - ga)
    rlo, rhi = pl.ds(0, ra), pl.ds(ra, bs - ra)
    ly, lg, lr, lm = Lane(cs, cr), Lane(gs, gr), Lane(rs, rr), Lane(ms, mr)

    def at(dy=0, dk=0, dz=0, dx=0):
        return {
            "row": ((y + dy) % ny) * 2 + (k + dk) % 2,
            "col": ((z + dz) % nz) * nx + (x + dx) % nx,
        }

    here = at()
    loads = [
        pltpu.make_async_copy(a, b, lsem.at[i])
        for i, (a, b) in enumerate([
            (panel_hbm, panel), (rows_hbm, rows), (cols_hbm, cols), (blocks_hbm, B), (previous_hbm, previous),
        ])
    ]
    loads[0].start()
    peers = [at(dk=1)]
    peers += [at(dy=d) for d in range(1, ny)]
    peers += [at(dz=NR * d) for d in range(1, ns)]
    peers += [at(dz=1), at(dz=-1)]
    peers += [at(dx=d) for d in range(1, nx)]
    barrier = pltpu.get_barrier_semaphore()
    for dev in peers:
        pl.semaphore_signal(barrier, inc=1, device_id=dev, device_id_type=MESH)
    for cp in loads[1:]:
        cp.start()
    loads[0].wait()
    own = panel[...]
    mine = C.at[k * ny + y]
    C[k * ny + y] = own
    G[zr, slot, x] = own.astype(F32).T.astype(BF)
    pl.semaphore_wait(barrier, len(peers))

    ownt = G.at[zr, slot, x]
    first = {d: lg.send(ownt, ownt, at(dz=NR * d)) for d in range(1, ns, 2)}
    for d in range(1, ny):
        ly.send(mine, mine, at(dy=d))
    ly.send(mine, mine, at(dk=1))

    def spread(piece):
        return (
            [lg.send(piece, piece, at(dz=dz)) for dz in (1, -1)],
            [lg.send(piece, piece, at(dx=d)) for d in range(1, nx)],
        )

    near = [spread(ownt)]
    first.update({d: lg.send(ownt, ownt, at(dz=NR * d)) for d in range(2, ns, 2)})

    D[slots] = jnp.zeros(D.shape[1:], F32)
    M[slots] = jnp.zeros(M.shape[1:], F32)
    tabv[...] = jnp.zeros(tabv.shape, I32)
    for cp in loads[1:3]:
        cp.wait()
    shift = nx.bit_length() - 1
    r = rows[...]
    rz = lax.shift_right_logical(r, shift)
    rzs = lax.shift_right_logical(rz * 11, 5)
    rk = (rz - rzs * NR) * ns + (rzs & 1) * h + lax.shift_right_logical(rzs, 1)
    rk = rk * nx + (r & (nx - 1))
    c = cols[...]
    ck = (c & 1) * ny + lax.shift_right_logical(c, 1)
    square = (slots, slots)
    t_of = lax.broadcasted_iota(I32, square, 0)
    s_of = lax.broadcasted_iota(I32, square, 1)
    alive = t_of < count[0, 0]
    tabv[0:1, 0:slots] = rk
    tabv[1:2, 0:slots] = ck
    for i, key in ((2, rk), (4, ck)):
        wide = jnp.broadcast_to(key, square)
        tall = wide.T
        before = jnp.max(jnp.where((tall == wide) & (t_of < s_of), t_of, -1), axis=0, keepdims=True)
        last = jnp.max(jnp.where((tall == s_of) & alive, t_of, -1), axis=0, keepdims=True)
        tabv[i : i + 1, 0:slots] = jnp.where(before < 0, slots, before)
        tabv[i + 1 : i + 2, 0:slots] = jnp.where(last < 0, slots, last)
    table_copy = pltpu.make_async_copy(tabv, tab, lsem.at[5])
    table_copy.start()

    for d in range(1, ns, 2):
        lg.got(ownt, first[d], here)
    near.append(spread(G.at[zr, pl.ds((1 - par) * h, h), x]))

    def slots_of(source, kind):
        szs = source // NR
        spar, spair = szs % 2, szs // 2
        start = (spar * h + spair, (1 - spar) * h, spar * h + 1 - spair)[kind]
        return pl.ds(start, h if kind == 1 else 1)

    corner = []

    def corners(kind):
        like = G.at[zr, slots_of(z, kind), x]
        for e, dz in enumerate((1, -1)):
            lg.got(like, near[kind][0][e], here)
            source = (z + nz - dz) % nz
            part = G.at[source % NR, slots_of(source, kind), x, lo]
            for d in range(1, nx):
                corner.append((part, lg.send(part, part, at(dx=d))))
        for d in range(1, nx):
            lg.got(like, near[kind][1][d - 1], here)
            part = G.at[zr, slots_of(z, kind), (x + nx - d) % nx, hi]
            for dz in (1, -1):
                corner.append((part, lg.send(part, part, at(dz=dz))))

    corners(0)
    if ns > 2:
        for d in range(2, ns, 2):
            lg.got(ownt, first[d], here)
        near.append(spread(G.at[zr, slots_of(z, 2), x]))

    for d in range(1, ny):
        ly.got(mine, d - 1, here)
        there = C.at[k * ny + (y + ny - d) % ny]
        ly.send(there, there, at(dk=1))
    corners(1)

    table_copy.wait()
    loads[3].wait()
    for i in range(ny - 1, 2 * ny - 1):
        ly.got(mine, i, here)

    def direct(s, carry):
        D[s] = jnp.dot(B[s], C[tab[1, s]], preferred_element_type=F32) + D[tab[2, s]]
        return carry

    lax.fori_loop(0, slots, direct, 0, unroll=UNROLL)

    def round_rows(i, carry):
        T[i // (ns * nx), (i // nx) % ns, i % nx] = D[tab[3, i]].astype(BF)
        return carry

    lax.fori_loop(0, nz * nx, round_rows, 0, unroll=8)
    if ns > 2:
        corners(2)
    stage = []
    for p in range(2):
        part = pl.ds(p * h, h)
        stage.append((
            [lr.send(T.at[:, part, (x + d) % nx, rlo], RXA.at[d - 1, :, part], at(dx=d)) for d in range(1, nx)],
            [
                lr.send(T.at[q, part, :, rhi], RZB.at[e, part], at(dz=dz))
                for e, (q, dz) in enumerate(((zp, 1), (zm, -1)))
            ],
        ))

    for like, i in corner:
        lg.got(like, i, here)

    def mirror(s, carry):
        t = tab[0, s]
        p = G[lax.div(t, ns * nx), lax.rem(lax.div(t, nx), ns), lax.rem(t, nx)]
        M[s] = jnp.dot(p, B[s], preferred_element_type=F32) + M[tab[4, s]]
        return carry

    lax.fori_loop(0, slots, mirror, 0, unroll=UNROLL)

    def round_other(i, carry):
        MS[i] = M[tab[5, (1 - k) * ny + i]].astype(BF)
        return carry

    lax.fori_loop(0, ny, round_other, 0, unroll=8)
    swap = lm.send(MS, MR, at(dk=1))

    second = []

    def sums(p):
        part = pl.ds(p * h, h)
        for e in range(2):
            lr.got(RZB.at[e, part], stage[p][1][e], here)

        def sum_b(i, carry):
            s, w = p * h + i // nx, i % nx
            total = D[tab[3, (zr * ns + s) * nx + w]][ra:]
            total = total + RZB[0, s, w].astype(F32) + RZB[1, s, w].astype(F32)
            SB[w, s] = total.astype(BF)
            return carry

        lax.fori_loop(0, h * nx, sum_b, 0, unroll=4)
        over_x = [lr.send(SB.at[(x + d) % nx, part], RXB.at[d - 1, part], at(dx=d)) for d in range(1, nx)]
        for d in range(1, nx):
            lr.got(RXA.at[d - 1, :, part], stage[p][0][d - 1], here)

        def sum_a(i, carry):
            q, s = i // h, p * h + i % h
            total = D[tab[3, (q * ns + s) * nx + x]][:ra]
            for d in range(1, nx):
                total = total + RXA[d - 1, q, s].astype(F32)
            SA[q, s] = total.astype(BF)
            return carry

        lax.fori_loop(0, NR * h, sum_a, 0, unroll=NR)
        over_z = [
            lr.send(SA.at[q, part], RZA.at[e, part], at(dz=dz)) for e, (q, dz) in enumerate(((zp, 1), (zm, -1)))
        ]
        second.append((over_x, over_z))

    sums(0)

    lm.got(MR, swap, here)

    def sum_m(i, carry):
        N[i] = (M[tab[5, k * ny + i]] + MR[i].astype(F32)).astype(BF)
        return carry

    lax.fori_loop(0, ny, sum_m, 0, unroll=8)
    over_y = [lm.send(N.at[(y + d) % ny], YR.at[d - 1], at(dy=d)) for d in range(1, ny)]
    sums(1)

    third = []
    for d in range(1, ns):
        to = (zs + d) % ns
        third.append((to, *lr.make(SH.at[(to % 2) * h + to // 2], R3.at[d - 1], at(dz=NR * d))))
    for p in range(2):
        part = pl.ds(p * h, h)
        over_x, over_z = second[p]
        for e in range(2):
            lr.got(RZA.at[e, part], over_z[e], here)
        for d in range(1, nx):
            lr.got(RXB.at[d - 1, part], over_x[d - 1], here)
        for j in range(h):
            s = p * h + j
            a = SA[zr, s].astype(F32) + RZA[0, s].astype(F32) + RZA[1, s].astype(F32)
            b = SB[x, s].astype(F32)
            for d in range(1, nx):
                b = b + RXB[d - 1, s].astype(F32)
            S3[s, :ra] = a
            S3[s, ra:] = b
            SH[s, :ra] = a.astype(BF)
            SH[s, ra:] = b.astype(BF)
        for to, _, cp in third:
            pl.when(to % 2 == p)(cp.start)

    total = M[tab[5, k * ny + y]] + MR[y].astype(F32)
    for d in range(1, ny):
        lm.got(YR.at[d - 1], over_y[d - 1], here)
        total = total + YR[d - 1].astype(F32)
    for cp in loads[4:]:
        cp.wait()
    product = total.T + S3[slot]
    scale = 2.0 / jnp.full((bs, bs), width[0], F32)
    moved = center[0] * panel[...].astype(F32)
    before = previous[...].astype(F32)
    for d in range(1, ns):
        lr.got(R3.at[d - 1], third[d - 1][1], here)
        product = product + R3[d - 1].astype(F32)
    out[...] = (scale * (product - moved) - before).astype(BF)
    for lane in (ly, lg, lr, lm):
        lane.drain()


def body(nx, panel, previous, blocks, block_rows, block_cols, counts, center, half_width):
    bs = panel.shape[0]
    ny = lax.axis_size("row") // 2
    ns = lax.axis_size("col") // nx // NR
    slots = blocks.shape[2]
    ra, rb = REDUCE_ROWS, bs - REDUCE_ROWS
    hbm = pl.BlockSpec(memory_space=pltpu.HBM)
    dma = pltpu.SemaphoreType.DMA
    vmem = pltpu.VMEM
    gathers = (ns - 1) + min(ns, 3) * (nx + 1 + 4 * (nx - 1))
    reduces = 4 * (nx + 1) + ns - 1
    return pl.pallas_call(
        functools.partial(kernel, nx, ny, ns),
        name="filter_step",
        out_shape=jax.ShapeDtypeStruct((bs, bs), BF),
        in_specs=[pl.BlockSpec(memory_space=pltpu.SMEM)] * 3 + [hbm] * 5,
        out_specs=pl.BlockSpec(memory_space=pltpu.VMEM),
        scratch_shapes=[
            vmem((bs, bs), BF),
            vmem((bs, bs), BF),
            vmem((slots, bs, bs), BF),
            vmem((1, slots), I32),
            vmem((1, slots), I32),
            vmem((8, 128), I32),
            pltpu.SMEM((8, 128), I32),
            vmem((2 * ny, bs, bs), BF),
            vmem((NR, ns, nx, bs, bs), BF),
            vmem((slots + 1, bs, bs), F32),
            vmem((slots + 1, bs, bs), F32),
            vmem((NR, ns, nx, bs, bs), BF),
            vmem((nx - 1, NR, ns, ra, bs), BF),
            vmem((2, ns, nx, rb, bs), BF),
            vmem((2, ns, ra, bs), BF),
            vmem((nx - 1, ns, rb, bs), BF),
            vmem((NR, ns, ra, bs), BF),
            vmem((nx, ns, rb, bs), BF),
            vmem((ns, bs, bs), F32),
            vmem((ns, bs, bs), BF),
            vmem((ns - 1, bs, bs), BF),
            vmem((ny, bs, bs), BF),
            vmem((ny, bs, bs), BF),
            vmem((ny, bs, bs), BF),
            vmem((ny - 1, bs, bs), BF),
            dma((6,)),
            dma((2 * ny - 1,)), dma((2 * ny - 1,)),
            dma((gathers,)), dma((gathers,)),
            dma((reduces,)), dma((reduces,)),
            dma((ny,)), dma((ny,)),
        ],
        compiler_params=pltpu.CompilerParams(
            collective_id=0, has_side_effects=True, vmem_limit_bytes=60 << 20
        ),
    )(
        counts, center, half_width, panel, previous, blocks.reshape(slots, bs, bs),
        block_rows.reshape(1, slots), block_cols.reshape(1, slots),
    )


def solution(mesh):
    placed = (
        P(("row", "col"), None),
        P(("row", "col"), None),
        P("row", "col", None, None, None),
        P("row", "col", None),
        P("row", "col", None),
        P("row", "col"),
        P(),
        P(),
    )
    return jax.shard_map(
        functools.partial(body, NX), mesh=mesh, in_specs=placed, out_specs=P(("row", "col"), None), check_vma=False
    )
```

time: 661 us -> 56.1 us (0.08)
  the two profiles are of different devices: /device:TPU:1 before, /device:TPU:40 now
where the time goes in v2:
time: 56.1 us; the launch traced here: 55.8 us
  Pallas kernels  52.5 us (94%)
  between operations  1.95 us (3%)
  local copies, waits for them, and re-layouts  1.38 us (2%)
    pallas_call x1, Pallas kernels, body(): pl.pallas_call(functools.partial(kernel, nx, ny, ns), name='filter_step',...  52.5 us
    unnamed x1, local copies, waits for them, and re-layouts  1.38 us

profile of v2, /device:TPU:40, one launch (start us, length us, event | category | flops | bytes accessed | tf_op | source)
XLA Modules:
  0.0 55.8 jit_solution(15533087369862715492)
XLA Ops:
  1.9 52.5 %filter_step.1 = bf16[128,128]{1,0:T(8,128)(2,1)} custom-call(s32[1,1]{1,0:T(1,128)S(6)} %copy.10.count, f32[1]{0:T(128)S(6)} %copy.11.center, f32[1]{0:T(128)S(6)} %copy.12.width, bf16[128,128]{1,0:T(8,128)(2,1)} %panel_hbm.1, bf16[128,128]{1,0:T(8,128)(2,1)} %previous_hbm.1, bf16[64,128,128]{2,1,0:T(8,128)(2,1)} %bitcast.3, s32[1,64]{1,0:T(1,128)} %bitcast.4, ...), custom_call_target="tpu_custom_call" | custom-call | tf_op jit(solution)/shard_map/filter_step/pallas_call | solution.py:329
  54.4 1.4 %copy.13 = bf16[128,128]{1,0:T(8,128)(2,1)} copy(bf16[128,128]{1,0:T(8,128)(2,1)} %filter_step.1) | data formatting | bytes 65536

commit v3 on v2

--- a/solution.py
+++ b/solution.py
@@ -14,7 +14,7 @@
 NX = 4
 NR = 3
 GATHER_ROWS = 64
-REDUCE_ROWS = 48
+PIECES = ((16, 32), (16, 32), (16, 16))
 UNROLL = 32
 
 
@@ -60,12 +60,15 @@
     h = ns // 2
     par, pair = zs % 2, zs // 2
     slot = par * h + pair
+    place = lambda zs: (zs % 2) * h + zs // 2
     slots = B.shape[0]
     bs = panel.shape[0]
     zm, zp = (zr + NR - 1) % NR, (zr + 1) % NR
-    ga, ra = GATHER_ROWS, REDUCE_ROWS
-    lo, hi = pl.ds(0, ga), pl.ds(ga, bs - ga)
-    rlo, rhi = pl.ds(0, ra), pl.ds(ra, bs - ra)
+    lo, hi = pl.ds(0, GATHER_ROWS), pl.ds(GATHER_ROWS, bs - GATHER_ROWS)
+    spans, start = [], 0
+    for a, b in PIECES:
+        spans.append((pl.ds(start, a), pl.ds(start + a, b), pl.ds(start, a + b)))
+        start += a + b
     ly, lg, lr, lm = Lane(cs, cr), Lane(gs, gr), Lane(rs, rr), Lane(ms, mr)
 
     def at(dy=0, dk=0, dz=0, dx=0):
@@ -101,9 +104,6 @@
 
     ownt = G.at[zr, slot, x]
     first = {d: lg.send(ownt, ownt, at(dz=NR * d)) for d in range(1, ns, 2)}
-    for d in range(1, ny):
-        ly.send(mine, mine, at(dy=d))
-    ly.send(mine, mine, at(dk=1))
 
     def spread(piece):
         return (
@@ -113,6 +113,9 @@
 
     near = [spread(ownt)]
     first.update({d: lg.send(ownt, ownt, at(dz=NR * d)) for d in range(2, ns, 2)})
+    for d in range(1, ny):
+        ly.send(mine, mine, at(dy=d))
+    ly.send(mine, mine, at(dk=1))
 
     D[slots] = jnp.zeros(D.shape[1:], F32)
     M[slots] = jnp.zeros(M.shape[1:], F32)
@@ -192,20 +195,23 @@
 
     lax.fori_loop(0, slots, direct, 0, unroll=UNROLL)
 
-    def round_rows(i, carry):
-        T[i // (ns * nx), (i // nx) % ns, i % nx] = D[tab[3, i]].astype(BF)
-        return carry
-
-    lax.fori_loop(0, nz * nx, round_rows, 0, unroll=8)
     if ns > 2:
         corners(2)
     stage = []
-    for p in range(2):
-        part = pl.ds(p * h, h)
+    for over_x, over_z, both in spans:
+
+        def round_rows(i, carry):
+            T[i // (ns * nx), (i // nx) % ns, i % nx, both] = D[tab[3, i], both].astype(BF)
+            return carry
+
+        lax.fori_loop(0, nz * nx, round_rows, 0, unroll=8)
         stage.append((
-            [lr.send(T.at[:, part, (x + d) % nx, rlo], RXA.at[d - 1, :, part], at(dx=d)) for d in range(1, nx)],
             [
-                lr.send(T.at[q, part, :, rhi], RZB.at[e, part], at(dz=dz))
+                lr.send(T.at[:, :, (x + d) % nx, over_x], RXA.at[d - 1, :, :, over_x], at(dx=d))
+                for d in range(1, nx)
+            ],
+            [
+                lr.send(T.at[q, :, :, over_z], RZB.at[e, :, :, over_z], at(dz=dz))
                 for e, (q, dz) in enumerate(((zp, 1), (zm, -1)))
             ],
         ))
@@ -231,35 +237,38 @@
     second = []
 
     def sums(p):
-        part = pl.ds(p * h, h)
+        over_x, over_z, _ = spans[p]
         for e in range(2):
-            lr.got(RZB.at[e, part], stage[p][1][e], here)
+            lr.got(RZB.at[e, :, :, over_z], stage[p][1][e], here)
 
         def sum_b(i, carry):
-            s, w = p * h + i // nx, i % nx
-            total = D[tab[3, (zr * ns + s) * nx + w]][ra:]
-            total = total + RZB[0, s, w].astype(F32) + RZB[1, s, w].astype(F32)
-            SB[w, s] = total.astype(BF)
+            s, w = i // nx, i % nx
+            total = D[tab[3, (zr * ns + s) * nx + w], over_z]
+            total = total + RZB[0, s, w, over_z].astype(F32) + RZB[1, s, w, over_z].astype(F32)
+            SB[w, s, over_z] = total.astype(BF)
             return carry
 
-        lax.fori_loop(0, h * nx, sum_b, 0, unroll=4)
-        over_x = [lr.send(SB.at[(x + d) % nx, part], RXB.at[d - 1, part], at(dx=d)) for d in range(1, nx)]
+        lax.fori_loop(0, ns * nx, sum_b, 0, unroll=4)
+        to_x = [
+            lr.send(SB.at[(x + d) % nx, :, over_z], RXB.at[d - 1, :, over_z], at(dx=d)) for d in range(1, nx)
+        ]
         for d in range(1, nx):
-            lr.got(RXA.at[d - 1, :, part], stage[p][0][d - 1], here)
+            lr.got(RXA.at[d - 1, :, :, over_x], stage[p][0][d - 1], here)
 
         def sum_a(i, carry):
-            q, s = i // h, p * h + i % h
-            total = D[tab[3, (q * ns + s) * nx + x]][:ra]
+            q, s = i // ns, i % ns
+            total = D[tab[3, i * nx + x], over_x]
             for d in range(1, nx):
-                total = total + RXA[d - 1, q, s].astype(F32)
-            SA[q, s] = total.astype(BF)
+                total = total + RXA[d - 1, q, s, over_x].astype(F32)
+            SA[q, s, over_x] = total.astype(BF)
             return carry
 
-        lax.fori_loop(0, NR * h, sum_a, 0, unroll=NR)
-        over_z = [
-            lr.send(SA.at[q, part], RZA.at[e, part], at(dz=dz)) for e, (q, dz) in enumerate(((zp, 1), (zm, -1)))
+        lax.fori_loop(0, NR * ns, sum_a, 0, unroll=4)
+        to_z = [
+            lr.send(SA.at[q, :, over_x], RZA.at[e, :, over_x], at(dz=dz))
+            for e, (q, dz) in enumerate(((zp, 1), (zm, -1)))
         ]
-        second.append((over_x, over_z))
+        second.append((to_x, to_z))
 
     sums(0)
 
@@ -271,31 +280,27 @@
 
     lax.fori_loop(0, ny, sum_m, 0, unroll=8)
     over_y = [lm.send(N.at[(y + d) % ny], YR.at[d - 1], at(dy=d)) for d in range(1, ny)]
-    sums(1)
+    for p in range(1, len(spans)):
+        sums(p)
 
     third = []
-    for d in range(1, ns):
-        to = (zs + d) % ns
-        third.append((to, *lr.make(SH.at[(to % 2) * h + to // 2], R3.at[d - 1], at(dz=NR * d))))
-    for p in range(2):
-        part = pl.ds(p * h, h)
-        over_x, over_z = second[p]
+    for p, (over_x, over_z, both) in enumerate(spans):
         for e in range(2):
-            lr.got(RZA.at[e, part], over_z[e], here)
+            lr.got(RZA.at[e, :, over_x], second[p][1][e], here)
         for d in range(1, nx):
-            lr.got(RXB.at[d - 1, part], over_x[d - 1], here)
-        for j in range(h):
-            s = p * h + j
-            a = SA[zr, s].astype(F32) + RZA[0, s].astype(F32) + RZA[1, s].astype(F32)
-            b = SB[x, s].astype(F32)
+            lr.got(RXB.at[d - 1, :, over_z], second[p][0][d - 1], here)
+        for s in range(ns):
+            a = SA[zr, s, over_x].astype(F32) + RZA[0, s, over_x].astype(F32) + RZA[1, s, over_x].astype(F32)
+            b = SB[x, s, over_z].astype(F32)
             for d in range(1, nx):
-                b = b + RXB[d - 1, s].astype(F32)
-            S3[s, :ra] = a
-            S3[s, ra:] = b
-            SH[s, :ra] = a.astype(BF)
-            SH[s, ra:] = b.astype(BF)
-        for to, _, cp in third:
-            pl.when(to % 2 == p)(cp.start)
+                b = b + RXB[d - 1, s, over_z].astype(F32)
+            S3[s, over_x] = a
+            S3[s, over_z] = b
+            SH[s, over_x] = a.astype(BF)
+            SH[s, over_z] = b.astype(BF)
+        third.append([
+            lr.send(SH.at[place((zs + d) % ns), both], R3.at[d - 1, both], at(dz=NR * d)) for d in range(1, ns)
+        ])
 
     total = M[tab[5, k * ny + y]] + MR[y].astype(F32)
     for d in range(1, ny):
@@ -303,14 +308,16 @@
         total = total + YR[d - 1].astype(F32)
     for cp in loads[4:]:
         cp.wait()
-    product = total.T + S3[slot]
+    mirrored = total.T
     scale = 2.0 / jnp.full((bs, bs), width[0], F32)
-    moved = center[0] * panel[...].astype(F32)
-    before = previous[...].astype(F32)
-    for d in range(1, ns):
-        lr.got(R3.at[d - 1], third[d - 1][1], here)
-        product = product + R3[d - 1].astype(F32)
-    out[...] = (scale * (product - moved) - before).astype(BF)
+    for p, (_, _, both) in enumerate(spans):
+        rows_of = slice(both.start, both.start + both.size)
+        product = mirrored[rows_of] + S3[slot, both]
+        product = product - center[0] * panel[both].astype(F32)
+        for d in range(1, ns):
+            lr.got(R3.at[d - 1, both], third[p][d - 1], here)
+            product = product + R3[d - 1, both].astype(F32)
+        out[both] = (scale[rows_of] * product - previous[both].astype(F32)).astype(BF)
     for lane in (ly, lg, lr, lm):
         lane.drain()
 
@@ -320,12 +327,11 @@
     ny = lax.axis_size("row") // 2
     ns = lax.axis_size("col") // nx // NR
     slots = blocks.shape[2]
-    ra, rb = REDUCE_ROWS, bs - REDUCE_ROWS
     hbm = pl.BlockSpec(memory_space=pltpu.HBM)
     dma = pltpu.SemaphoreType.DMA
     vmem = pltpu.VMEM
     gathers = (ns - 1) + min(ns, 3) * (nx + 1 + 4 * (nx - 1))
-    reduces = 4 * (nx + 1) + ns - 1
+    reduces = len(PIECES) * (2 * (nx + 1) + ns - 1)
     return pl.pallas_call(
         functools.partial(kernel, nx, ny, ns),
         name="filter_step",
@@ -345,12 +351,12 @@
             vmem((slots + 1, bs, bs), F32),
             vmem((slots + 1, bs, bs), F32),
             vmem((NR, ns, nx, bs, bs), BF),
-            vmem((nx - 1, NR, ns, ra, bs), BF),
-            vmem((2, ns, nx, rb, bs), BF),
-            vmem((2, ns, ra, bs), BF),
-            vmem((nx - 1, ns, rb, bs), BF),
-            vmem((NR, ns, ra, bs), BF),
-            vmem((nx, ns, rb, bs), BF),
+            vmem((nx - 1, NR, ns, bs, bs), BF),
+            vmem((2, ns, nx, bs, bs), BF),
+            vmem((2, ns, bs, bs), BF),
+            vmem((nx - 1, ns, bs, bs), BF),
+            vmem((NR, ns, bs, bs), BF),
+            vmem((nx, ns, bs, bs), BF),
             vmem((ns, bs, bs), F32),
             vmem((ns, bs, bs), BF),
             vmem((ns - 1, bs, bs), BF),

time: 56.1 us -> 57.4 us (1.023)
  the two profiles are of different devices: /device:TPU:40 before, /device:TPU:1 now
where the time goes in v3:
time: 57.4 us; the launch traced here: 56.5 us
  Pallas kernels  53.2 us (93%)
  between operations  1.95 us (3%)
  local copies, waits for them, and re-layouts  1.38 us (2%)
    pallas_call x1, Pallas kernels, body(): pl.pallas_call(functools.partial(kernel, nx, ny, ns), name='filter_step',...  53.2 us
    unnamed x1, local copies, waits for them, and re-layouts  1.38 us

profile of v3, /device:TPU:1, one launch (start us, length us, event | category | flops | bytes accessed | tf_op | source)
XLA Modules:
  0.0 56.5 jit_solution(2242477534967445802)
XLA Ops:
  1.9 53.2 %filter_step.1 = bf16[128,128]{1,0:T(8,128)(2,1)} custom-call(s32[1,1]{1,0:T(1,128)S(6)} %copy.10.count, f32[1]{0:T(128)S(6)} %copy.11.center, f32[1]{0:T(128)S(6)} %copy.12.width, bf16[128,128]{1,0:T(8,128)(2,1)} %panel_hbm.1, bf16[128,128]{1,0:T(8,128)(2,1)} %previous_hbm.1, bf16[64,128,128]{2,1,0:T(8,128)(2,1)} %bitcast.3, s32[1,64]{1,0:T(1,128)} %bitcast.4, ...), custom_call_target="tpu_custom_call" | custom-call | tf_op jit(solution)/shard_map/filter_step/pallas_call | solution.py:335
  55.2 1.4 %copy.13 = bf16[128,128]{1,0:T(8,128)(2,1)} copy(bf16[128,128]{1,0:T(8,128)(2,1)} %filter_step.1) | data formatting | bytes 65536

commit v4 on v2

--- a/solution.py
+++ b/solution.py
@@ -221,12 +221,16 @@
 
     lax.fori_loop(0, slots, mirror, 0, unroll=UNROLL)
 
+    other = (pl.ds(0, ny // 2), pl.ds(ny // 2, ny - ny // 2))
+
     def round_other(i, carry):
-        MS[i] = M[tab[5, (1 - k) * ny + i]].astype(BF)
-        return carry
-
-    lax.fori_loop(0, ny, round_other, 0, unroll=8)
-    swap = lm.send(MS, MR, at(dk=1))
+        MS[i] = M[tab[5, (1 - k) * ny + lax.rem(y + i + 1, ny)]].astype(BF)
+        return carry
+
+    swap = []
+    for part in other:
+        lax.fori_loop(part.start, part.start + part.size, round_other, 0, unroll=part.size)
+        swap.append(lm.send(MS.at[part], MR.at[part], at(dk=1)))
 
     second = []
 
@@ -261,16 +265,17 @@
         ]
         second.append((over_x, over_z))
 
+    def sum_m(i, carry):
+        N[i] = (M[tab[5, k * ny + lax.rem(y + i + 1, ny)]] + MR[i].astype(F32)).astype(BF)
+        return carry
+
+    over_y = []
+    for part, i in zip(other, swap):
+        lm.got(MR.at[part], i, here)
+        lax.fori_loop(part.start, part.start + part.size, sum_m, 0, unroll=part.size)
+        for d in range(part.start + 1, min(part.start + part.size, ny - 1) + 1):
+            over_y.append(lm.send(N.at[d - 1], YR.at[d - 1], at(dy=d)))
     sums(0)
-
-    lm.got(MR, swap, here)
-
-    def sum_m(i, carry):
-        N[i] = (M[tab[5, k * ny + i]] + MR[i].astype(F32)).astype(BF)
-        return carry
-
-    lax.fori_loop(0, ny, sum_m, 0, unroll=8)
-    over_y = [lm.send(N.at[(y + d) % ny], YR.at[d - 1], at(dy=d)) for d in range(1, ny)]
     sums(1)
 
     third = []
@@ -297,7 +302,7 @@
         for to, _, cp in third:
             pl.when(to % 2 == p)(cp.start)
 
-    total = M[tab[5, k * ny + y]] + MR[y].astype(F32)
+    total = M[tab[5, k * ny + y]] + MR[ny - 1].astype(F32)
     for d in range(1, ny):
         lm.got(YR.at[d - 1], over_y[d - 1], here)
         total = total + YR[d - 1].astype(F32)
@@ -362,7 +367,7 @@
             dma((2 * ny - 1,)), dma((2 * ny - 1,)),
             dma((gathers,)), dma((gathers,)),
             dma((reduces,)), dma((reduces,)),
-            dma((ny,)), dma((ny,)),
+            dma((ny + 1,)), dma((ny + 1,)),
         ],
         compiler_params=pltpu.CompilerParams(
             collective_id=0, has_side_effects=True, vmem_limit_bytes=60 << 20

time: 56.1 us -> 56.4 us (level)
  the two profiles are of different devices: /device:TPU:40 before, /device:TPU:1 now
where the time goes in v4:
time: 56.4 us; the launch traced here: 55.6 us
  Pallas kernels  52.2 us (93%)
  between operations  1.95 us (3%)
  local copies, waits for them, and re-layouts  1.38 us (2%)
    pallas_call x1, Pallas kernels, body(): pl.pallas_call(functools.partial(kernel, nx, ny, ns), name='filter_step',...  52.2 us
    unnamed x1, local copies, waits for them, and re-layouts  1.38 us

profile of v4, /device:TPU:1, one launch (start us, length us, event | category | flops | bytes accessed | tf_op | source)
XLA Modules:
  0.0 55.6 jit_solution(396652662894545852)
XLA Ops:
  1.9 52.2 %filter_step.1 = bf16[128,128]{1,0:T(8,128)(2,1)} custom-call(s32[1,1]{1,0:T(1,128)S(6)} %copy.10.count, f32[1]{0:T(128)S(6)} %copy.11.center, f32[1]{0:T(128)S(6)} %copy.12.width, bf16[128,128]{1,0:T(8,128)(2,1)} %panel_hbm.1, bf16[128,128]{1,0:T(8,128)(2,1)} %previous_hbm.1, bf16[64,128,128]{2,1,0:T(8,128)(2,1)} %bitcast.3, s32[1,64]{1,0:T(1,128)} %bitcast.4, ...), custom_call_target="tpu_custom_call" | custom-call | tf_op jit(solution)/shard_map/filter_step/pallas_call | solution.py:334
  54.2 1.4 %copy.13 = bf16[128,128]{1,0:T(8,128)(2,1)} copy(bf16[128,128]{1,0:T(8,128)(2,1)} %filter_step.1) | data formatting | bytes 65536

commit v5 on v4

--- a/solution.py
+++ b/solution.py
@@ -75,6 +75,12 @@
         }
 
     here = at()
+
+    def nearest(n):
+        return sorted(range(1, n), key=lambda d: min(d, n - d))
+
+    near_x, near_y = nearest(nx), nearest(ny)
+    far_x, far_y = near_x[::-1], near_y[::-1]
     loads = [
         pltpu.make_async_copy(a, b, lsem.at[i])
         for i, (a, b) in enumerate([
@@ -101,14 +107,13 @@
 
     ownt = G.at[zr, slot, x]
     first = {d: lg.send(ownt, ownt, at(dz=NR * d)) for d in range(1, ns, 2)}
-    for d in range(1, ny):
-        ly.send(mine, mine, at(dy=d))
-    ly.send(mine, mine, at(dk=1))
+    along_y = {d: ly.send(mine, mine, at(dy=d)) for d in far_y}
+    across = [ly.send(mine, mine, at(dk=1))]
 
     def spread(piece):
         return (
             [lg.send(piece, piece, at(dz=dz)) for dz in (1, -1)],
-            [lg.send(piece, piece, at(dx=d)) for d in range(1, nx)],
+            {d: lg.send(piece, piece, at(dx=d)) for d in far_x},
         )
 
     near = [spread(ownt)]
@@ -161,10 +166,10 @@
             lg.got(like, near[kind][0][e], here)
             source = (z + nz - dz) % nz
             part = G.at[source % NR, slots_of(source, kind), x, lo]
-            for d in range(1, nx):
+            for d in far_x:
                 corner.append((part, lg.send(part, part, at(dx=d))))
-        for d in range(1, nx):
-            lg.got(like, near[kind][1][d - 1], here)
+        for d in near_x:
+            lg.got(like, near[kind][1][d], here)
             part = G.at[zr, slots_of(z, kind), (x + nx - d) % nx, hi]
             for dz in (1, -1):
                 corner.append((part, lg.send(part, part, at(dz=dz))))
@@ -175,15 +180,15 @@
             lg.got(ownt, first[d], here)
         near.append(spread(G.at[zr, slots_of(z, 2), x]))
 
-    for d in range(1, ny):
-        ly.got(mine, d - 1, here)
+    for d in near_y:
+        ly.got(mine, along_y[d], here)
         there = C.at[k * ny + (y + ny - d) % ny]
-        ly.send(there, there, at(dk=1))
+        across.append(ly.send(there, there, at(dk=1)))
     corners(1)
 
     table_copy.wait()
     loads[3].wait()
-    for i in range(ny - 1, 2 * ny - 1):
+    for i in across:
         ly.got(mine, i, here)
 
     def direct(s, carry):
@@ -203,7 +208,7 @@
     for p in range(2):
         part = pl.ds(p * h, h)
         stage.append((
-            [lr.send(T.at[:, part, (x + d) % nx, rlo], RXA.at[d - 1, :, part], at(dx=d)) for d in range(1, nx)],
+            {d: lr.send(T.at[:, part, (x + d) % nx, rlo], RXA.at[d - 1, :, part], at(dx=d)) for d in far_x},
             [
                 lr.send(T.at[q, part, :, rhi], RZB.at[e, part], at(dz=dz))
                 for e, (q, dz) in enumerate(((zp, 1), (zm, -1)))
@@ -247,9 +252,9 @@
             return carry
 
         lax.fori_loop(0, h * nx, sum_b, 0, unroll=4)
-        over_x = [lr.send(SB.at[(x + d) % nx, part], RXB.at[d - 1, part], at(dx=d)) for d in range(1, nx)]
+        over_x = {d: lr.send(SB.at[(x + d) % nx, part], RXB.at[d - 1, part], at(dx=d)) for d in far_x}
         for d in range(1, nx):
-            lr.got(RXA.at[d - 1, :, part], stage[p][0][d - 1], here)
+            lr.got(RXA.at[d - 1, :, part], stage[p][0][d], here)
 
         def sum_a(i, carry):
             q, s = i // h, p * h + i % h
@@ -269,12 +274,13 @@
         N[i] = (M[tab[5, k * ny + lax.rem(y + i + 1, ny)]] + MR[i].astype(F32)).astype(BF)
         return carry
 
-    over_y = []
+    over_y = {}
     for part, i in zip(other, swap):
         lm.got(MR.at[part], i, here)
         lax.fori_loop(part.start, part.start + part.size, sum_m, 0, unroll=part.size)
-        for d in range(part.start + 1, min(part.start + part.size, ny - 1) + 1):
-            over_y.append(lm.send(N.at[d - 1], YR.at[d - 1], at(dy=d)))
+        for d in far_y:
+            if part.start < d <= part.start + part.size:
+                over_y[d] = lm.send(N.at[d - 1], YR.at[d - 1], at(dy=d))
     sums(0)
     sums(1)
 
@@ -288,7 +294,7 @@
         for e in range(2):
             lr.got(RZA.at[e, part], over_z[e], here)
         for d in range(1, nx):
-            lr.got(RXB.at[d - 1, part], over_x[d - 1], here)
+            lr.got(RXB.at[d - 1, part], over_x[d], here)
         for j in range(h):
             s = p * h + j
             a = SA[zr, s].astype(F32) + RZA[0, s].astype(F32) + RZA[1, s].astype(F32)
@@ -304,7 +310,7 @@
 
     total = M[tab[5, k * ny + y]] + MR[ny - 1].astype(F32)
     for d in range(1, ny):
-        lm.got(YR.at[d - 1], over_y[d - 1], here)
+        lm.got(YR.at[d - 1], over_y[d], here)
         total = total + YR[d - 1].astype(F32)
     for cp in loads[4:]:
         cp.wait()

time: 56.4 us -> 56.2 us (level); the launches traced: 55.6 us -> 56 us
  no operation moved by 1% of the time
where the time goes in v5:
time: 56.2 us; the launch traced here: 56 us
  Pallas kernels  52.7 us (94%)
  between operations  1.95 us (3%)
  local copies, waits for them, and re-layouts  1.38 us (2%)
    pallas_call x1, Pallas kernels, body(): pl.pallas_call(functools.partial(kernel, nx, ny, ns), name='filter_step',...  52.7 us
    unnamed x1, local copies, waits for them, and re-layouts  1.38 us

profile of v5, /device:TPU:1, one launch (start us, length us, event | category | flops | bytes accessed | tf_op | source)
XLA Modules:
  0.0 56.0 jit_solution(11623093298738691962)
XLA Ops:
  1.9 52.7 %filter_step.1 = bf16[128,128]{1,0:T(8,128)(2,1)} custom-call(s32[1,1]{1,0:T(1,128)S(6)} %copy.10.count, f32[1]{0:T(128)S(6)} %copy.11.center, f32[1]{0:T(128)S(6)} %copy.12.width, bf16[128,128]{1,0:T(8,128)(2,1)} %panel_hbm.1, bf16[128,128]{1,0:T(8,128)(2,1)} %previous_hbm.1, bf16[64,128,128]{2,1,0:T(8,128)(2,1)} %bitcast.3, s32[1,64]{1,0:T(1,128)} %bitcast.4, ...), custom_call_target="tpu_custom_call" | custom-call | tf_op jit(solution)/shard_map/filter_step/pallas_call | solution.py:340
  54.6 1.4 %copy.13 = bf16[128,128]{1,0:T(8,128)(2,1)} copy(bf16[128,128]{1,0:T(8,128)(2,1)} %filter_step.1) | data formatting | bytes 65536
